TPU v7x, 32 devices: a whole 2x2x4 slice. The times are simulated.
32 devices in a mesh: clips: 2 (over y), tm: 4 (over x, core), rows: 4 (over z).
Axes of the slice: x: 2, y: 2, z: 4, core: 2. Of those that a mesh axis runs over, the one named last changes fastest.
Arguments:
- features: bfloat16 [8, 8, 48, 384], P(('clips', 'tm'), 'rows'), parts along dimension 0, may hold values from -320 to 320
- first_gain: float32 [384], replicated, may hold values from 0.5 to 1.5
- first_shift: float32 [384], replicated, may hold values from -3 to 3
- first_kernel: bfloat16 [384, 3, 3, 3, 384], P('tm'), may hold values from -0.0625 to 0.0625
- first_bias: float32 [384], P('tm'), may hold values from -2 to 2
- second_gain: float32 [384], replicated, may hold values from 0.5 to 1.5
- second_shift: float32 [384], replicated, may hold values from -3 to 3
- second_kernel: bfloat16 [384, 3, 3, 3, 384], P('tm'), may hold values from -0.0625 to 0.0625
- second_bias: float32 [384], P('tm'), may hold values from -2 to 2
- third_gain: float32 [384], replicated, may hold values from 0.5 to 1.5
- third_shift: float32 [384], replicated, may hold values from -3 to 3
- query_weight: bfloat16 [384, 384], replicated, may hold values from -0.30618622 to 0.30618622
- key_weight: bfloat16 [384, 384], replicated, may hold values from -1.8371173 to 1.8371173
- value_weight: bfloat16 [384, 384], replicated, may hold values from -0.3125 to 0.3125
- output_weight: bfloat16 [384, 384], replicated, may hold values from -0.3125 to 0.3125
Outputs:
- decoded: bfloat16 [8, 8, 48, 384], P(('clips', 'tm'), 'rows'), parts along dimension 0
There are 2 independent parts, one for each index of `clips`. A program takes and returns all parts, laid end to end along the dimension named above; an argument that names none is the same for every part. Nothing has to cross between parts.
All inputs are finite; a program needn't handle non-finite values.
Results may differ from a plain program's by a relative error of at most 0.029.
Values may be sent and summed in bfloat16 or wider, within the bound.
A program may use at most 64 MiB of HBM per device.

v0:
```python
import jax
import jax.numpy as jnp
from jax import lax
from jax.sharding import PartitionSpec as P

C = 384
GROUPS = 32


epsilon = 1e-06


def extended(cells, sides, width):
    for axis, dim in sides:
        count = lax.axis_size(axis)
        ends = count - 1
        head = lax.slice_in_dim(cells, 0, width, axis=dim)
        tail = lax.slice_in_dim(cells, cells.shape[dim] - width, cells.shape[dim], axis=dim)
        cells = jnp.concatenate(
            [
                lax.ppermute(tail, axis, [(i, (i + 1) % count) for i in range(ends)]),
                cells,
                lax.ppermute(head, axis, [((i + 1) % count, i) for i in range(ends)]),
            ],
            axis=dim,
        )
    return cells


def group_norm(values, gain, shift):
    frame_count, row_count, col_count, channels = values.shape
    entries = lax.axis_size("rows") * row_count * col_count * (channels // GROUPS)
    grouped = values.reshape(frame_count, row_count, col_count, GROUPS, channels // GROUPS)
    sums = lax.psum(jnp.sum(grouped, axis=(1, 2, 4)), "rows")
    average = sums / entries
    centered = grouped - average[:, None, None, :, None]
    variance = lax.psum(jnp.sum(centered * centered, axis=(1, 2, 4)), "rows") / entries
    scaled = centered * lax.rsqrt(variance + epsilon)[:, None, None, :, None]
    return scaled.reshape(frame_count, row_count, col_count, channels) * gain + shift


def causal_conv(active, kernel, bias):
    widened = extended(active, (("rows", 1),), 1)
    clip_frames = lax.all_gather(widened, "tm", axis=0, tiled=True)
    frame_count, padded_rows, col_count, channels = clip_frames.shape
    row_count = padded_rows - 2
    outputs = kernel.shape[0]
    padded = jnp.pad(clip_frames, ((2, 0), (0, 0), (1, 1), (0, 0)))
    summed = jnp.zeros((outputs, frame_count * row_count * col_count), jnp.float32)
    for tap_time in range(3):
        for tap_row in range(3):
            window = padded[tap_time : tap_time + frame_count, tap_row : tap_row + row_count]
            stacked = jnp.concatenate(
                [window[:, :, shift_col : shift_col + col_count] for shift_col in range(3)], axis=-1
            )
            tap_weight = kernel[:, tap_time, tap_row].reshape(outputs, 3 * channels)
            summed = summed + lax.dot_general(
                tap_weight,
                stacked.reshape(-1, 3 * channels),
                (((1,), (1,)), ((), ())),
                preferred_element_type=jnp.float32,
            )
    result = (
        (summed + bias[:, None])
        .astype(jnp.bfloat16)
        .reshape(outputs, frame_count, row_count, col_count)
    )
    mixed = lax.all_to_all(result, "tm", split_axis=1, concat_axis=0, tiled=True)
    return jnp.transpose(mixed, (1, 2, 3, 0))


def absorb(carry, queries, keys, values):
    peak, total, summed = carry
    scores = jnp.einsum("fqc,fkc->fqk", queries, keys, preferred_element_type=jnp.float32)
    new_peak = jnp.max(scores, axis=-1)
    factor = jnp.exp(peak - new_peak)
    expon = jnp.exp(scores - new_peak[..., None])
    total = total * factor + jnp.sum(expon, axis=-1)
    summed = summed * factor[..., None] + jnp.einsum(
        "fqk,fkc->fqc", expon.astype(jnp.bfloat16), values, preferred_element_type=jnp.float32
    )
    return (new_peak, total, summed)


def per_device(
    features,
    first_gain,
    first_shift,
    first_kernel,
    first_bias,
    second_gain,
    second_shift,
    second_kernel,
    second_bias,
    third_gain,
    third_shift,
    query_weight,
    key_weight,
    value_weight,
    output_weight,
):
    frame_count, row_count, col_count, channels = features.shape
    start = features.astype(jnp.float32)
    active1 = jax.nn.silu(group_norm(start, first_gain, first_shift)).astype(jnp.bfloat16)
    conv1 = causal_conv(active1, first_kernel, first_bias)
    active2 = jax.nn.silu(group_norm(conv1.astype(jnp.float32), second_gain, second_shift)).astype(
        jnp.bfloat16
    )
    conv2 = causal_conv(active2, second_kernel, second_bias)
    hidden = (start + conv2.astype(jnp.float32)).astype(jnp.bfloat16)
    normed = group_norm(hidden.astype(jnp.float32), third_gain, third_shift).astype(jnp.bfloat16)
    flat = normed.reshape(frame_count, row_count * col_count, channels)
    queries = (
        jnp.einsum("fpc,cd->fpd", flat, query_weight, preferred_element_type=jnp.float32)
        * C ** (-0.5)
    ).astype(jnp.bfloat16)
    positions = row_count * col_count
    initial = (
        jnp.full((frame_count, positions), -jnp.inf, jnp.float32),
        jnp.zeros((frame_count, positions), jnp.float32),
        jnp.zeros((frame_count, positions, channels), jnp.float32),
    )
    keys = jnp.einsum("fpc,cd->fpd", flat, key_weight, preferred_element_type=jnp.float32).astype(
        jnp.bfloat16
    )
    values = jnp.einsum(
        "fpc,cd->fpd", flat, value_weight, preferred_element_type=jnp.float32
    ).astype(jnp.bfloat16)
    shape4 = (frame_count, row_count, col_count, channels)
    peak, total, summed = absorb(
        initial,
        queries,
        lax.all_gather(keys.reshape(shape4), "rows", axis=1, tiled=True).reshape(
            frame_count, -1, channels
        ),
        lax.all_gather(values.reshape(shape4), "rows", axis=1, tiled=True).reshape(
            frame_count, -1, channels
        ),
    )
    attended = (summed / total[..., None]).astype(jnp.bfloat16)
    projected = jnp.einsum(
        "fpc,cd->fpd", attended, output_weight, preferred_element_type=jnp.float32
    )
    decoded = hidden.astype(jnp.float32) + projected.reshape(
        frame_count, row_count, col_count, channels
    )
    return decoded.astype(jnp.bfloat16)


def solution(mesh):
    in_specs = (
        P(("clips", "tm"), "rows", None, None),
        P(),
        P(),
        P("tm", None, None, None, None),
        P("tm"),
        P(),
        P(),
        P("tm", None, None, None, None),
        P("tm"),
        P(),
        P(),
        P(),
        P(),
        P(),
        P(),
    )
    out_specs = P(("clips", "tm"), "rows", None, None)
    return jax.shard_map(
        per_device, mesh=mesh, in_specs=in_specs, out_specs=out_specs, check_vma=False
    )
```

profile of v0, /device:TPU:0, one launch (start us, length us, event | category | flops | bytes accessed | tf_op | source)
XLA Modules:
  0.0 157.3 jit_solution(10581170224222182222)
XLA Ops:
  0.0 1.0 convert_reduce_fusion.1
  1.2 13.5 %psum.42 = f32[1,32]{1,0:T(1,128)S(1)} all-reduce(f32[1,32]{1,0:T(1,128)S(1)} %bitcast.277), channel_id=1, replica_groups=mesh['clips'=2,'tm'=4,'rows'=4] {'rows'}, use_global_device_ids=true, to_apply=%region_2.0 | all-reduce | flops 32 | bytes 256 | tf_op jit(solution)/shard_map/psum | solution.py:34
  14.8 0.9 fusion.21
  16.0 8.4 %psum.43 = f32[1,32]{1,0:T(1,128)S(1)} all-reduce(f32[1,32]{1,0:T(1,128)S(1)} %bitcast.278), channel_id=1, replica_groups=mesh['clips'=2,'tm'=4,'rows'=4] {'rows'}, use_global_device_ids=true, to_apply=%region_5.6 | all-reduce | flops 32 | bytes 256 | tf_op jit(solution)/shard_map/psum | solution.py:37
  24.5 1.0 fusion.29
  25.5 3.9 %collective-permute-start = (bf16[1,1,48,384]{3,2,1,0:T(8,128)(2,1)S(1)}, bf16[1,1,48,384]{3,2,1,0:T(8,128)(2,1)S(1)}, u32[]{:S(2)}, u32[]{:S(2)}) collective-permute-start(bf16[1,1,48,384]{3,2,1,0:T(8,128)(2,1)S(1)} %get-tuple-element.81), channel_id=1, source_target_pairs={{0,1},{1,2},{2,3},{4,5},{5,6},{6,7},{8,9},{9,10},{10,11},{12,13},{... | collective-permute-start | bytes 110600 | tf_op jit(solution)/shard_map/ppermute | solution.py:21
  29.4 1.3 collective-permute-start.1
  30.7 1.8 %fusion.45 = (bf16[96,1,1,3,384]{4,0,3,2,1:T(8,128)(2,1)S(1)}, bf16[96,1,1,3,384]{4,0,3,2,1:T(8,128)(2,1)S(1)}, bf16[96,1,1,3,384]{4,0,3,2,1:T(8,128)(2,1)S(1)},...) fusion(bf16[96,3,3,3,384]{4,0,3,2,1:T(8,128)(2,1)} %param.18), kind=kLoop, calls=%fused_computation.150 | loop fusion | bytes 3981312 | tf_op jit(solution)/shard_map/slice | solution.py:56
  34.3 1.0 collective-permute-done.1
  35.3 7.5 %all_gather.12 = bf16[4,4,48,384]{3,2,1,0:T(8,128)(2,1)S(1)} all-gather(bf16[1,4,48,384]{3,2,1,0:T(8,128)(2,1)S(1)} %pad_maximum_fusion.18), channel_id=1, replica_groups=mesh['clips'=2,'tm'=4,'rows'=4] {'tm'}, dimensions={0}, use_global_device_ids=true | all-gather | bytes 737280 | tf_op jit(solution)/shard_map/all_gather | solution.py:44
  42.8 1.8 %pad_slice_fusion.25 = (bf16[4,2,48,384]{3,2,1,0:T(8,128)(2,1)S(1)}, bf16[4,2,48,384]{3,2,1,0:T(8,128)(2,1)S(1)}, bf16[4,2,48,384]{3,2,1,0:T(8,128)(2,1)S(1)}, b...) fusion(bf16[4,4,48,384]{3,2,1,0:T(8,128)(2,1)S(1)} %all_gather.12), kind=kLoop, calls=%fused_computation.25 | loop fusion | bytes 6193152 | tf_op jit(solution)/shard_map/slice | solution.py:54
  49.7 6.7 %all_to_all.8 = bf16[96,4,2,48]{0,3,2,1:T(8,128)(2,1)S(1)} all-to-all(bf16[96,4,2,48]{0,3,2,1:T(8,128)(2,1)S(1)} %bitcast.270), channel_id=1, replica_groups=mesh['clips'=2,'tm'=4,'rows'=4] {'tm'}, dimensions={1} | all-to-all | bytes 147456 | tf_op jit(solution)/shard_map/all_to_all | solution.py:68
  56.9 10.1 %psum.44 = f32[1,32]{1,0:T(1,128)S(1)} all-reduce(f32[1,32]{1,0:T(1,128)S(1)} %bitcast.279), channel_id=1, replica_groups=mesh['clips'=2,'tm'=4,'rows'=4] {'rows'}, use_global_device_ids=true, to_apply=%region_8.9 | all-reduce | flops 32 | bytes 256 | tf_op jit(solution)/shard_map/psum | solution.py:34
  67.5 8.7 %psum.45 = f32[1,32]{1,0:T(1,128)S(1)} all-reduce(f32[1,32]{1,0:T(1,128)S(1)} %bitcast.280), channel_id=1, replica_groups=mesh['clips'=2,'tm'=4,'rows'=4] {'rows'}, use_global_device_ids=true, to_apply=%region_11.12 | all-reduce | flops 32 | bytes 256 | tf_op jit(solution)/shard_map/psum | solution.py:37
  76.4 3.6 %collective-permute-start.2 = (bf16[1,1,48,384]{3,2,1,0:T(8,128)(2,1)S(1)}, bf16[1,1,48,384]{3,2,1,0:T(8,128)(2,1)S(1)}, u32[]{:S(2)}, u32[]{:S(2)}) collective-permute-start(bf16[1,1,48,384]{3,2,1,0:T(8,128)(2,1)S(1)} %get-tuple-element.79), channel_id=1, source_target_pairs={{0,1},{1,2},{2,3},{4,5},{5,6},{6,7},{8,9},{9,10},{10,11},{12,13},{... | collective-permute-start | bytes 110600 | tf_op jit(solution)/shard_map/ppermute | solution.py:21
  80.0 1.3 collective-permute-start.3
  83.3 2.5 %collective-permute-done.3 = bf16[1,1,48,384]{3,2,1,0:T(8,128)(2,1)S(1)} collective-permute-done((bf16[1,1,48,384]{3,2,1,0:T(8,128)(2,1)S(1)}, bf16[1,1,48,384]{3,2,1,0:T(8,128)(2,1)S(1)}, u32[]{:S(2)}, u32[]{:S(2)}) %collective-permute-start.3) | collective-permute-done | bytes 36896 | tf_op jit(solution)/shard_map/ppermute | solution.py:23
  85.9 6.9 %all_gather.13 = bf16[4,4,48,384]{3,2,1,0:T(8,128)(2,1)S(1)} all-gather(bf16[1,4,48,384]{3,2,1,0:T(8,128)(2,1)S(1)} %pad_maximum_fusion.19), channel_id=1, replica_groups=mesh['clips'=2,'tm'=4,'rows'=4] {'tm'}, dimensions={0}, use_global_device_ids=true | all-gather | bytes 737280 | tf_op jit(solution)/shard_map/all_gather | solution.py:44
  92.8 1.7 %pad_slice_fusion.1 = (bf16[4,2,48,384]{3,2,1,0:T(8,128)(2,1)S(1)}, bf16[4,2,48,384]{3,2,1,0:T(8,128)(2,1)S(1)}, bf16[4,2,48,384]{3,2,1,0:T(8,128)(2,1)S(1)}, bf...) fusion(bf16[4,4,48,384]{3,2,1,0:T(8,128)(2,1)S(1)} %all_gather.13), kind=kLoop, calls=%fused_computation.1 | loop fusion | bytes 6193152 | tf_op jit(solution)/shard_map/slice | solution.py:54
  99.5 6.7 %all_to_all.9 = bf16[96,4,2,48]{0,3,2,1:T(8,128)(2,1)S(1)} all-to-all(bf16[96,4,2,48]{0,3,2,1:T(8,128)(2,1)S(1)} %bitcast.271), channel_id=1, replica_groups=mesh['clips'=2,'tm'=4,'rows'=4] {'tm'}, dimensions={1} | all-to-all | bytes 147456 | tf_op jit(solution)/shard_map/all_to_all | solution.py:68
  106.8 8.5 %psum.46 = f32[1,32]{1,0:T(1,128)S(1)} all-reduce(f32[1,32]{1,0:T(1,128)S(1)} %bitcast.281), channel_id=1, replica_groups=mesh['clips'=2,'tm'=4,'rows'=4] {'rows'}, use_global_device_ids=true, to_apply=%region_14.15 | all-reduce | flops 32 | bytes 256 | tf_op jit(solution)/shard_map/psum | solution.py:34
  115.8 10.2 %psum.47 = f32[1,32]{1,0:T(1,128)S(1)} all-reduce(f32[1,32]{1,0:T(1,128)S(1)} %bitcast.276), channel_id=1, replica_groups=mesh['clips'=2,'tm'=4,'rows'=4] {'rows'}, use_global_device_ids=true, to_apply=%region_17.18 | all-reduce | flops 32 | bytes 256 | tf_op jit(solution)/shard_map/psum | solution.py:37
  126.5 14.7 %all_gather.14 = bf16[1,8,48,384]{3,2,0,1:T(8,128)(2,1)S(1)} all-gather(bf16[1,2,48,384]{3,2,0,1:T(8,128)(2,1)S(1)} %bitcast.274), channel_id=1, replica_groups=mesh['clips'=2,'tm'=4,'rows'=4] {'rows'}, dimensions={1}, use_global_device_ids=true | all-gather | bytes 368640 | tf_op jit(solution)/shard_map/all_gather | solution.py:133
  142.1 14.1 %all_gather.15 = bf16[1,8,48,384]{3,2,0,1:T(8,128)(2,1)S(1)} all-gather(bf16[1,2,48,384]{3,2,0,1:T(8,128)(2,1)S(1)} %bitcast.273), channel_id=1, replica_groups=mesh['clips'=2,'tm'=4,'rows'=4] {'rows'}, dimensions={1}, use_global_device_ids=true | all-gather | bytes 368640 | tf_op jit(solution)/shard_map/all_gather | solution.py:136
  (152 shorter events, 18.8 us)
Async XLA Ops:
  0.0 141.2 %copy-start = (bf16[384,384]{1,0:T(8,128)(2,1)S(1)}, bf16[384,384]{1,0:T(8,128)(2,1)}, u32[]{:S(2)}) copy-start(bf16[384,384]{1,0:T(8,128)(2,1)} %param.26) | copy-start | bytes 884740
  25.5 8.8 %collective-permute-start = (bf16[1,1,48,384]{3,2,1,0:T(8,128)(2,1)S(1)}, bf16[1,1,48,384]{3,2,1,0:T(8,128)(2,1)S(1)}, u32[]{:S(2)}, u32[]{:S(2)}) collective-permute-start(bf16[1,1,48,384]{3,2,1,0:T(8,128)(2,1)S(1)} %get-tuple-element.81), channel_id=1, source_target_pairs={{0,1},{1,2},{2,3},{4,5},{5,6},{6,7},{8,9},{9,10},{10,11},{12,13},{... | collective-permute-start | bytes 110600 | tf_op jit(solution)/shard_map/ppermute | solution.py:21
  29.4 5.9 %collective-permute-start.1 = (bf16[1,1,48,384]{3,2,1,0:T(8,128)(2,1)S(1)}, bf16[1,1,48,384]{3,2,1,0:T(8,128)(2,1)S(1)}, u32[]{:S(2)}, u32[]{:S(2)}) collective-permute-start(bf16[1,1,48,384]{3,2,1,0:T(8,128)(2,1)S(1)} %get-tuple-element.82), channel_id=1, source_target_pairs={{1,0},{2,1},{3,2},{5,4},{6,5},{7,6},{9,8},{10,9},{11,10},{13,12},{... | collective-permute-start | bytes 110600 | tf_op jit(solution)/shard_map/ppermute | solution.py:23
  48.5 0.7 copy-start.10
  49.0 27.3 %copy-start.6 = (f32[384]{0:T(512)S(1)}, f32[384]{0:T(512)}, u32[]{:S(2)}) copy-start(f32[384]{0:T(512)} %param.21) | copy-start | bytes 4612
  49.0 27.3 %copy-start.7 = (f32[384]{0:T(512)S(1)}, f32[384]{0:T(512)}, u32[]{:S(2)}) copy-start(f32[384]{0:T(512)} %param.20) | copy-start | bytes 4612
  49.0 32.3 %copy-start.1 = (bf16[96,3,3,3,384]{4,0,3,2,1:T(8,128)(2,1)S(1)}, bf16[96,3,3,3,384]{4,0,3,2,1:T(8,128)(2,1)}, u32[]{:S(2)}) copy-start(bf16[96,3,3,3,384]{4,0,3,2,1:T(8,128)(2,1)} %param.22) | copy-start | bytes 5971972
  76.4 6.9 %collective-permute-start.2 = (bf16[1,1,48,384]{3,2,1,0:T(8,128)(2,1)S(1)}, bf16[1,1,48,384]{3,2,1,0:T(8,128)(2,1)S(1)}, u32[]{:S(2)}, u32[]{:S(2)}) collective-permute-start(bf16[1,1,48,384]{3,2,1,0:T(8,128)(2,1)S(1)} %get-tuple-element.79), channel_id=1, source_target_pairs={{0,1},{1,2},{2,3},{4,5},{5,6},{6,7},{8,9},{9,10},{10,11},{12,13},{... | collective-permute-start | bytes 110600 | tf_op jit(solution)/shard_map/ppermute | solution.py:21
  80.0 5.9 %collective-permute-start.3 = (bf16[1,1,48,384]{3,2,1,0:T(8,128)(2,1)S(1)}, bf16[1,1,48,384]{3,2,1,0:T(8,128)(2,1)S(1)}, u32[]{:S(2)}, u32[]{:S(2)}) collective-permute-start(bf16[1,1,48,384]{3,2,1,0:T(8,128)(2,1)S(1)} %get-tuple-element.80), channel_id=1, source_target_pairs={{1,0},{2,1},{3,2},{5,4},{6,5},{7,6},{9,8},{10,9},{11,10},{13,12},{... | collective-permute-start | bytes 110600 | tf_op jit(solution)/shard_map/ppermute | solution.py:23
  97.7 1.3 copy-start.11
  98.5 8.1 %copy-start.2 = (bf16[1,2,48,384]{3,2,1,0:T(8,128)(2,1)S(1)}, bf16[1,2,48,384]{3,2,1,0:T(8,128)(2,1)}, u32[]{:S(2)}) copy-start(bf16[1,2,48,384]{3,2,1,0:T(8,128)(2,1)} %param.15) | copy-start | bytes 221188
  98.9 27.3 %copy-start.8 = (f32[384]{0:T(512)S(1)}, f32[384]{0:T(512)}, u32[]{:S(2)}) copy-start(f32[384]{0:T(512)} %param.25) | copy-start | bytes 4612
  99.0 27.3 %copy-start.9 = (f32[384]{0:T(512)S(1)}, f32[384]{0:T(512)}, u32[]{:S(2)}) copy-start(f32[384]{0:T(512)} %param.24) | copy-start | bytes 4612
  99.0 27.4 %copy-start.3 = (bf16[384,384]{1,0:T(8,128)(2,1)S(1)}, bf16[384,384]{1,0:T(8,128)(2,1)}, u32[]{:S(2)}) copy-start(bf16[384,384]{1,0:T(8,128)(2,1)} %param.27) | copy-start | bytes 884740
  106.3 35.6 %copy-start.4 = (bf16[384,384]{1,0:T(8,128)(2,1)S(1)}, bf16[384,384]{1,0:T(8,128)(2,1)}, u32[]{:S(2)}) copy-start(bf16[384,384]{1,0:T(8,128)(2,1)} %param.28) | copy-start | bytes 884740
  126.3 30.1 %copy-start.5 = (bf16[384,384]{1,0:T(8,128)(2,1)S(1)}, bf16[384,384]{1,0:T(8,128)(2,1)}, u32[]{:S(2)}) copy-start(bf16[384,384]{1,0:T(8,128)(2,1)} %param.29) | copy-start | bytes 884740
where the time goes:
time: 158 us; the launch traced here: 157 us
  blocking collectives  116 us (73%)
  local copies, waits for them, and re-layouts  12.1 us (8%)
  starting transfers between devices  10.1 us (6%)
  matrix products  9.27 us (6%)
  other arithmetic  5.53 us (4%)
  waiting for transfers between devices  3.52 us (2%)
    psum x3, blocking collectives, group_norm(): sums = lax.psum(jnp.sum(grouped, axis=(1, 2, 4)), 'rows')  32.1 us
    psum x3, blocking collectives, group_norm(): lax.psum(jnp.sum(centered * centered, axis=(1, 2, 4)), 'rows') / entries  27.3 us
    all_gather x1, blocking collectives, per_device(): lax.all_gather(keys.reshape(shape4), 'rows', axis=1, tiled=True)  14.7 us
    all_gather x2, blocking collectives, causal_conv(): clip_frames = lax.all_gather(widened, 'tm', axis=0, tiled=True)  14.4 us
    all_gather x1, blocking collectives, per_device(): lax.all_gather(values.reshape(shape4), 'rows', axis=1, tiled=True)  14.1 us
    all_to_all x2, blocking collectives, causal_conv(): lax.all_to_all(result, 'tm', split_axis=1, concat_axis=0, tiled=True)  13.4 us
    ppermute x2, starting transfers between devices, extended(): lax.ppermute(tail, axis, [(i, (i + 1) % count) for i in range(ends)])  7.47 us
    dot_general x18, matrix products, causal_conv(): lax.dot_general(tap_weight, stacked.reshape(-1, 3 * channels), (((1,), (1...  7.32 us
  transfers between devices with their start and end apart: 4, of which 2 were waited for; matrix products, arithmetic and copies ran while one was open for 3% of the time, Pallas kernels for 0%

commit v1 on v0

v1 whole, which is shorter than its diff:
```python
import functools

import jax
import jax.numpy as jnp
from jax import lax
from jax.experimental import pallas as pl
from jax.experimental.pallas import tpu as pltpu
from jax.sharding import PartitionSpec as P

GROUPS = 32
EPS = 1e-06
LANES = 128
MESH = pl.DeviceIdType.MESH
F32 = jnp.float32
BF16 = jnp.bfloat16
NT = (((1,), (1,)), ((), ()))


def each(count, body):
    if count <= 16:
        for n in range(count):
            body(n)
    else:
        lax.fori_loop(0, count, lambda n, c: (body(n), c)[1], 0)


def membership(size, per_group):
    a = lax.broadcasted_iota(jnp.int32, (size, size), 0) // per_group
    b = lax.broadcasted_iota(jnp.int32, (size, size), 1) // per_group
    return jnp.where(a == b, 1.0, 0.0).astype(BF16)


def group_sum(rows, member):
    hi = rows.astype(BF16).astype(F32)
    rest = rows - hi
    mid = rest.astype(BF16).astype(F32)
    low = rest - mid
    count = rows.shape[0]
    terms = jnp.concatenate([hi, mid, low], axis=0).astype(BF16)
    out = jnp.dot(terms, member, preferred_element_type=F32)
    return out[:count] + out[count : 2 * count] + out[2 * count :]


def block_stats(blocks, member, entries):
    sums = jnp.concatenate([jnp.sum(b, axis=0, keepdims=True) for b in blocks], axis=0)
    means = group_sum(sums, member) / entries
    squares = []
    for n, b in enumerate(blocks):
        d = b - means[n : n + 1]
        squares.append(jnp.sum(d * d, axis=0, keepdims=True))
    return means, group_sum(jnp.concatenate(squares, axis=0), member)


def merge_stats(means, squares, entries):
    count = len(means)
    mean = functools.reduce(lambda a, b: a + b, means) / count
    total = functools.reduce(lambda a, b: a + b, squares)
    for m in means:
        d = m - mean
        total = total + entries * (d * d)
    return mean, lax.rsqrt(total / (count * entries) + EPS)


def kernel(T, R, W, rows, C, OUT,
           feat, g1, s1, w1h, b1, g2, s2, w2h, b2, g3, s3, wqh, wkh, wvh, woh,
           out,
           xin, y1, cols, w1, w2, aw, st1, st2, hs, hfull, normed,
           lsem, blk_s, blk_r, top_s, top_r, bot_s, bot_r, st_s, st_r, hid_s, hid_r):
    t = lax.axis_index("tm")
    z = lax.axis_index("rows")
    me = t * R + z
    N = T * R
    RP = rows * W
    EXT = (rows + 2) * W
    per = C // GROUPS
    entries = RP * per

    loads = [
        pltpu.make_async_copy(w1h, w1.at[:, pl.ds(0, OUT), :], lsem.at[0]),
        pltpu.make_async_copy(w2h, w2.at[:, pl.ds(0, OUT), :], lsem.at[1]),
    ] + [
        pltpu.make_async_copy(src, aw.at[n], lsem.at[2 + n])
        for n, src in enumerate((wqh, wkh, wvh, woh))
    ]
    for load in loads:
        load.start()

    def peer(p):
        other = lax.rem(me + p, N)
        return other // R, lax.rem(other, R)

    barrier = pltpu.get_barrier_semaphore()

    def greet(n):
        pt, pz = peer(n + 1)
        pl.semaphore_signal(barrier, inc=1, device_id={"tm": pt, "rows": pz}, device_id_type=MESH)

    each(N - 1, greet)

    def remote(src, dst, ssem, rsem, pt, pz):
        return pltpu.make_async_remote_copy(
            src_ref=src, dst_ref=dst, send_sem=ssem, recv_sem=rsem,
            device_id={"tm": pt, "rows": pz}, device_id_type=MESH)

    x = feat[...].astype(F32)
    member = membership(C, per)
    mean, square = block_stats([x], member, entries)
    st1[me] = jnp.concatenate([mean, square], axis=0)
    if OUT < LANES:
        w1[:, OUT:, :] = jnp.zeros((27, LANES - OUT, C), BF16)
        w2[:, OUT:, :] = jnp.zeros((27, LANES - OUT, C), BF16)

    pl.semaphore_wait(barrier, N - 1)

    def stat_copy(phase, ref, n):
        pt, pz = peer(n + 1)
        return remote(ref.at[me], ref.at[me], st_s.at[phase, n], st_r.at[phase, me], pt, pz)

    def stat_arrival(phase, ref, n):
        pt, pz = peer(n + 1)
        src = pt * R + pz
        return remote(ref.at[src], ref.at[src], st_s.at[phase, n], st_r.at[phase, src], pt, pz)

    def gather_start(phase, body, first, last, at):
        def send_block(n):
            pt = lax.rem(t + n + 1, T)
            remote(body, at(t, W, RP), blk_s.at[phase, n], blk_r.at[phase, t], pt, z).start()

        def send_down(n):
            pt = lax.rem(t + n, T)
            remote(last, at(t, 0, W), top_s.at[phase, n], top_r.at[phase, t], pt, z + 1).start()

        def send_up(n):
            pt = lax.rem(t + n, T)
            remote(first, at(t, W + RP, W), bot_s.at[phase, n], bot_r.at[phase, t], pt, z - 1).start()

        each(T - 1, send_block)

        @pl.when(z + 1 < R)
        def _():
            each(T, send_down)

        @pl.when(z > 0)
        def _():
            each(T, send_up)

    def gather_sent(phase, body, first, last, at):
        each(T - 1, lambda n: remote(
            body, at(t, W, RP), blk_s.at[phase, n], blk_r.at[phase, t],
            lax.rem(t + n + 1, T), z).wait_send())

        @pl.when(z + 1 < R)
        def _():
            each(T, lambda n: remote(
                last, at(t, 0, W), top_s.at[phase, n], top_r.at[phase, t],
                lax.rem(t + n, T), z + 1).wait_send())

        @pl.when(z > 0)
        def _():
            each(T, lambda n: remote(
                first, at(t, W + RP, W), bot_s.at[phase, n], bot_r.at[phase, t],
                lax.rem(t + n, T), z - 1).wait_send())

    def block_wait(phase, at, n):
        src = lax.rem(t + n, T)
        remote(at(src, W, RP), at(src, W, RP), blk_s.at[phase, 0], blk_r.at[phase, src], src, z).wait_recv()

    def top_wait(phase, at, n):
        src = lax.rem(t + n, T)
        remote(at(src, 0, W), at(src, 0, W), top_s.at[phase, 0], top_r.at[phase, src], src, z - 1).wait_recv()

    def bot_wait(phase, at, n):
        src = lax.rem(t + n, T)
        remote(at(src, W + RP, W), at(src, W + RP, W), bot_s.at[phase, 0], bot_r.at[phase, src], src, z + 1).wait_recv()

    def put_columns(f, offset, value):
        count = value.shape[0]
        active = value * (0.5 * jnp.tanh(0.5 * value) + 0.5)
        col = lax.rem(lax.broadcasted_iota(jnp.int32, (count, C), 0), W)
        before = jnp.where(col == 0, 0.0, pltpu.roll(active, 1, 0))
        after = jnp.where(col == W - 1, 0.0, pltpu.roll(active, count - 1, 0))
        cols[f, pl.ds(offset, count), 0:C] = before.astype(BF16)
        cols[f, pl.ds(offset, count), C : 2 * C] = active.astype(BF16)
        cols[f, pl.ds(offset, count), 2 * C : 3 * C] = after.astype(BF16)

    def conv(weights):
        parts = {}
        for i in range(3):
            frames = T - (2 - i)
            if frames <= 0:
                continue
            total = None
            for j in range(3):
                for k in range(3):
                    window = cols[0:frames, j * W : j * W + RP, k * C : (k + 1) * C]
                    term = lax.dot_general(
                        window.reshape(frames * RP, C), weights[(i * 3 + j) * 3 + k], NT,
                        preferred_element_type=F32)
                    total = term if total is None else total + term
            parts[i] = total
        results = []
        for f in range(T):
            value = parts[2][f * RP : (f + 1) * RP]
            for i in (0, 1):
                src = f + i - 2
                if src >= 0:
                    value = value + parts[i][src * RP : (src + 1) * RP]
            results.append(value)
        return results

    zero_row = jnp.zeros((W, 3 * C), BF16)

    at1 = lambda src, offset, count: xin.at[src, pl.ds(offset, count), :]
    phase1 = (0, feat, feat.at[pl.ds(0, W), :], feat.at[pl.ds(RP - W, W), :], at1)
    each(N - 1, lambda n: stat_copy(0, st1, n).start())
    gather_start(*phase1)
    xin[t, W : W + RP, :] = feat[...]
    each(N - 1, lambda n: stat_arrival(0, st1, n).wait_recv())

    gain1, shift1 = g1[...], s1[...]

    def norm1(f):
        means = [st1[f * R + r, 0:1, :] for r in range(R)]
        squares = [st1[f * R + r, 1:2, :] for r in range(R)]
        mean, inv = merge_stats(means, squares, entries)
        return mean, inv * gain1

    def fill1(f, offset, count):
        mean, scale = norm1(f)
        value = (xin[f, pl.ds(offset, count), :].astype(F32) - mean) * scale + shift1
        put_columns(f, offset, value)

    def body1(n):
        if n > 0:
            block_wait(0, at1, n)
        fill1(lax.rem(t + n, T), W, RP)

    for n in range(T):
        body1(n)

    @pl.when(z > 0)
    def _():
        for n in range(T):
            top_wait(0, at1, n)
            fill1(lax.rem(t + n, T), 0, W)

    @pl.when(z == 0)
    def _():
        for f in range(T):
            cols[f, 0:W, :] = zero_row

    @pl.when(z + 1 < R)
    def _():
        for n in range(T):
            bot_wait(0, at1, n)
            fill1(lax.rem(t + n, T), W + RP, W)

    @pl.when(z + 1 == R)
    def _():
        for f in range(T):
            cols[f, W + RP : EXT, :] = zero_row

    loads[0].wait()
    bias1 = b1[...]
    outs = [(v + bias1).astype(BF16) for v in conv(w1)]
    member_out = membership(LANES, per)
    for f in range(T):
        y1[t, f, W : W + RP, :] = outs[f]
    mean, square = block_stats([v.astype(F32) for v in outs], member_out, entries)
    st2[me, 0] = mean
    st2[me, 1] = square

    at2 = lambda src, offset, count: y1.at[src, :, pl.ds(offset, count), :]
    phase2 = (1, at2(t, W, RP), at2(t, W, W), at2(t, RP, W), at2)
    each(N - 1, lambda n: stat_copy(1, st2, n).start())
    gather_start(*phase2)

    pick = jnp.where(
        (lax.broadcasted_iota(jnp.int32, (C, LANES), 0)
         == t * OUT + lax.broadcasted_iota(jnp.int32, (C, LANES), 1))
        & (lax.broadcasted_iota(jnp.int32, (C, LANES), 1) < OUT), 1.0, 0.0).astype(BF16)
    own = jnp.dot(xin[:, W : W + RP, :].reshape(T * RP, C), pick, preferred_element_type=F32)

    each(N - 1, lambda n: stat_arrival(1, st2, n).wait_recv())
    gain2, shift2 = g2[...], s2[...]
    mean_cols, inv_cols = [], []
    for s in range(T):
        mean, inv = merge_stats(
            [st2[s * R + r, 0] for r in range(R)], [st2[s * R + r, 1] for r in range(R)], entries)
        mean_cols.append(mean[:, :OUT])
        inv_cols.append(inv[:, :OUT])
    mean2 = jnp.concatenate(mean_cols, axis=1)
    scale2 = jnp.concatenate(inv_cols, axis=1) * gain2

    def joined(blocks):
        return jnp.concatenate([b.astype(F32)[:, :OUT] for b in blocks], axis=1)

    def fill2(f, offset, count):
        raw = joined([y1[s, f, offset : offset + count, :] for s in range(T)])
        value = (raw - mean2[f : f + 1]) * scale2[f : f + 1] + shift2
        put_columns(f, offset, value)

    for n in range(1, T):
        block_wait(1, at2, n)
    for f in range(T):
        fill2(f, W, RP)

    @pl.when(z > 0)
    def _():
        for n in range(T):
            top_wait(1, at2, n)
        for f in range(T):
            fill2(f, 0, W)

    @pl.when(z + 1 < R)
    def _():
        for n in range(T):
            bot_wait(1, at2, n)
        for f in range(T):
            fill2(f, W + RP, W)

    loads[1].wait()
    bias2 = b2[...]
    for f, v in enumerate(conv(w2)):
        rounded = (v + bias2).astype(BF16).astype(F32)
        hs[f] = (own[f * RP : (f + 1) * RP] + rounded).astype(BF16)

    def hidden_copy(n):
        pt, pz = peer(n + 1)
        return remote(hs.at[pt], hfull.at[t, pl.ds(z * RP, RP), :], hid_s.at[n], hid_r.at[me], pt, pz)

    def hidden_arrival(n):
        pt, pz = peer(n + 1)
        dst = hfull.at[pt, pl.ds(pz * RP, RP), :]
        return remote(dst, dst, hid_s.at[n], hid_r.at[pt * R + pz], pt, pz)

    each(N - 1, lambda n: hidden_copy(n).start())
    hfull[t, pl.ds(z * RP, RP), :] = hs[t]

    each(N - 1, lambda n: stat_copy(0, st1, n).wait_send())
    gather_sent(*phase1)
    each(N - 1, lambda n: stat_copy(1, st2, n).wait_send())
    gather_sent(*phase2)
    for n in range(2, 6):
        loads[n].wait()

    each(N - 1, lambda n: hidden_arrival(n).wait_recv())

    total_rows = R * RP
    chunk = min(total_rows, 4 * RP)
    parts = total_rows // chunk

    def frame_rows(n):
        start = pl.multiple_of(n * chunk, 16)
        return joined([hfull[s, pl.ds(start, chunk), :] for s in range(T)])

    def fold(body, init):
        if parts == 1:
            return body(0, init)
        return lax.fori_loop(0, parts, body, init)

    zero = jnp.zeros((1, C), F32)
    sums = fold(lambda n, a: a + jnp.sum(frame_rows(n), axis=0, keepdims=True), zero)
    mean = group_sum(sums, member) / (entries * R)

    def deviation(n, a):
        d = frame_rows(n) - mean
        return a + jnp.sum(d * d, axis=0, keepdims=True)

    var = group_sum(fold(deviation, zero), member) / (entries * R)
    scale3 = lax.rsqrt(var + EPS) * g3[...]
    shift3 = s3[...]

    def normalise(n, c):
        start = pl.multiple_of(n * chunk, 16)
        value = ((frame_rows(n) - mean) * scale3 + shift3).astype(BF16)
        normed[0, pl.ds(start, chunk), :] = value
        normed[1, pl.ds(start, chunk), :] = jnp.dot(value, aw[1], preferred_element_type=F32).astype(BF16)
        normed[2, pl.ds(start, chunk), :] = jnp.dot(value, aw[2], preferred_element_type=F32).astype(BF16)
        return c

    fold(normalise, 0)
    mine = pl.ds(pl.multiple_of(z * RP, 16), RP)
    queries = (jnp.dot(normed[0, mine, :], aw[0], preferred_element_type=F32) * C ** (-0.5)).astype(BF16)
    scores = lax.dot_general(queries, normed[1], NT, preferred_element_type=F32)
    peak = jnp.max(scores, axis=1, keepdims=True)
    weights = jnp.exp(scores - peak)
    total = jnp.sum(weights, axis=1, keepdims=True)
    summed = jnp.dot(weights.astype(BF16), normed[2], preferred_element_type=F32)
    attended = (summed / total).astype(BF16)
    hidden = joined([hfull[s, mine, :] for s in range(T)])
    out[...] = (hidden + jnp.dot(attended, aw[3], preferred_element_type=F32)).astype(BF16)

    each(N - 1, lambda n: hidden_copy(n).wait_send())


def solution(mesh):
    T, R = mesh.shape["tm"], mesh.shape["rows"]

    def per_device(features, g1, s1, k1, b1, g2, s2, k2, b2, g3, s3, wq, wk, wv, wo):
        _, rows, W, C = features.shape
        OUT = k1.shape[0]
        RP, EXT, N = rows * W, (rows + 2) * W, T * R
        vec = lambda a: a.reshape(1, -1)
        pad = lambda a: jnp.pad(a, (0, LANES - OUT)).reshape(1, LANES)
        taps = lambda k: jnp.transpose(k, (1, 2, 3, 0, 4)).reshape(27, OUT, C)
        vmem = pl.BlockSpec(memory_space=pltpu.VMEM)
        hbm = pl.BlockSpec(memory_space=pl.ANY)
        dma = pltpu.SemaphoreType.DMA
        result = pl.pallas_call(
            functools.partial(kernel, T, R, W, rows, C, OUT),
            out_shape=jax.ShapeDtypeStruct((RP, C), BF16),
            in_specs=[vmem, vmem, vmem, hbm, vmem, vmem, vmem, hbm, vmem, vmem, vmem, hbm, hbm, hbm, hbm],
            out_specs=vmem,
            scratch_shapes=[
                pltpu.VMEM((T, EXT, C), BF16),
                pltpu.VMEM((T, T, EXT, LANES), BF16),
                pltpu.VMEM((T, EXT, 3 * C), BF16),
                pltpu.VMEM((27, LANES, C), BF16),
                pltpu.VMEM((27, LANES, C), BF16),
                pltpu.VMEM((4, C, C), BF16),
                pltpu.VMEM((N, 2, C), F32),
                pltpu.VMEM((N, 2, T, LANES), F32),
                pltpu.VMEM((T, RP, LANES), BF16),
                pltpu.VMEM((T, R * RP, LANES), BF16),
                pltpu.VMEM((3, R * RP, C), BF16),
                dma((6,)),
                dma((2, T)), dma((2, T)),
                dma((2, T)), dma((2, T)),
                dma((2, T)), dma((2, T)),
                dma((2, N)), dma((2, N)),
                dma((N,)), dma((N,)),
            ],
            compiler_params=pltpu.CompilerParams(
                collective_id=0, has_side_effects=True, vmem_limit_bytes=48 * 1024 * 1024),
        )(features.reshape(RP, C), vec(g1), vec(s1), taps(k1), pad(b1), vec(g2), vec(s2),
          taps(k2), pad(b2), vec(g3), vec(s3), wq, wk, wv, wo)
        return result.reshape(features.shape)

    in_specs = (
        P(("clips", "tm"), "rows", None, None), P(), P(),
        P("tm", None, None, None, None), P("tm"), P(), P(),
        P("tm", None, None, None, None), P("tm"), P(), P(), P(), P(), P(), P(),
    )
    return jax.shard_map(
        per_device, mesh=mesh, in_specs=in_specs,
        out_specs=P(("clips", "tm"), "rows", None, None), check_vma=False)
```

time: 158 us -> 54 us (0.34)
  blocking collectives: 116 us -> 0 us
  Pallas kernels: 0 us -> 40.2 us
  starting transfers between devices: 10.1 us -> 0 us
  matrix products: 9.27 us -> 0 us
  other arithmetic: 5.53 us -> 0 us
  waiting for transfers between devices: 3.52 us -> 0 us
    psum x6 -> x0, blocking collectives: 59.3 us -> none  [the longest x3 32.1 us: group_norm(): sums = lax.psum(jnp.sum(grouped, axis=(1, 2, 4)), 'rows')]
    all_gather x4 -> x0, blocking collectives: 43.1 us -> none  [the longest x1 14.7 us: per_device(): lax.all_gather(keys.reshape(shape4), 'rows', axis=1, tiled=True)]
    pallas_call x0 -> x1, Pallas kernels: none -> 40.2 us  [per_device(): pl.pallas_call(functools.partial(kernel, T, R, W, rows, C, OUT), out_shap...]
    all_to_all x2 -> x0, blocking collectives: 13.4 us -> none  [causal_conv(): lax.all_to_all(result, 'tm', split_axis=1, concat_axis=0, tiled=True)]
    ppermute x4 -> x0, starting transfers between devices: 10.1 us -> none  [the longest x2 7.47 us: extended(): lax.ppermute(tail, axis, [(i, (i + 1) % count) for i in range(ends)])]
    dot_general x23 -> x0, matrix products: 9.27 us -> none  [the longest x18 7.32 us: causal_conv(): lax.dot_general(tap_weight, stacked.reshape(-1, 3 * channels), (((1,), (1...]
    slice x26 -> x0, local copies, waits for them, and re-layouts: 8.99 us -> none  [the longest x20 4.78 us: causal_conv(): tap_weight = kernel[:, tap_time, tap_row].reshape(outputs, 3 * channels)]
    unnamed x42 -> x15, local copies, waits for them, and re-layouts: 0.67 us -> 8.47 us
  transfers between devices with their start and end apart: 4 -> 0, of which waited for: 2 -> 0; matrix products, arithmetic and copies ran while one was open for 3% -> 0% of each run, Pallas kernels for 0% -> 0%
where the time goes in v1:
time: 54 us; the launch traced here: 53.5 us
  Pallas kernels  40.2 us (74%)
  local copies, waits for them, and re-layouts  13.2 us (24%)
    pallas_call x1, Pallas kernels, per_device(): pl.pallas_call(functools.partial(kernel, T, R, W, rows, C, OUT), out_shap...  40.2 us
    unnamed x15, local copies, waits for them, and re-layouts  8.47 us
    reshape x6, local copies, waits for them, and re-layouts, per_device(): vec = lambda a: a.reshape(1, -1)  4.1 us

profile of v1, /device:TPU:0, one launch (start us, length us, event | category | flops | bytes accessed | tf_op | source)
XLA Modules:
  0.0 53.5 jit_solution(5269571560515250366)
XLA Ops:
  0.0 0.7 %pad_bitcast_fusion = (f32[1,128]{1,0:T(1,128)S(1)}, f32[1,128]{1,0:T(1,128)S(1)}) fusion(f32[96]{0:T(128)} %param.23, f32[96]{0:T(128)} %param.19), kind=kLoop, calls=%fused_computation | loop fusion | bytes 1792 | tf_op jit(solution)/shard_map/reshape | solution.py:405
  0.7 0.7 %reshape.37.g1 = f32[1,384]{1,0:T(1,128)S(1)} reshape(f32[384]{0:T(512)} %param.16) | data formatting | bytes 3072 | tf_op jit(solution)/shard_map/reshape | solution.py:404
  1.4 0.7 %reshape.38.s1 = f32[1,384]{1,0:T(1,128)S(1)} reshape(f32[384]{0:T(512)} %param.17) | data formatting | bytes 3072 | tf_op jit(solution)/shard_map/reshape | solution.py:404
  2.0 0.7 %reshape.41.g2 = f32[1,384]{1,0:T(1,128)S(1)} reshape(f32[384]{0:T(512)} %param.20) | data formatting | bytes 3072 | tf_op jit(solution)/shard_map/reshape | solution.py:404
  2.7 0.7 %reshape.42.s2 = f32[1,384]{1,0:T(1,128)S(1)} reshape(f32[384]{0:T(512)} %param.21) | data formatting | bytes 3072 | tf_op jit(solution)/shard_map/reshape | solution.py:404
  3.4 0.7 %reshape.45.g3 = f32[1,384]{1,0:T(1,128)S(1)} reshape(f32[384]{0:T(512)} %param.24) | data formatting | bytes 3072 | tf_op jit(solution)/shard_map/reshape | solution.py:404
  4.1 0.7 %reshape.46.s3 = f32[1,384]{1,0:T(1,128)S(1)} reshape(f32[384]{0:T(512)} %param.25) | data formatting | bytes 3072 | tf_op jit(solution)/shard_map/reshape | solution.py:404
  4.8 0.0 copy-start
  4.8 1.6 %copy-done = bf16[96,3,3,3,384]{4,0,3,2,1:T(8,128)(2,1)S(1)} copy-done((bf16[96,3,3,3,384]{4,0,3,2,1:T(8,128)(2,1)S(1)}, bf16[96,3,3,3,384]{4,0,3,2,1:T(8,128)(2,1)}, u32[]{:S(2)}) %copy-start) | copy-done | bytes 1990680
  6.3 0.0 copy-start.1
  6.3 1.6 %copy-done.1 = bf16[96,3,3,3,384]{4,0,3,2,1:T(8,128)(2,1)S(1)} copy-done((bf16[96,3,3,3,384]{4,0,3,2,1:T(8,128)(2,1)S(1)}, bf16[96,3,3,3,384]{4,0,3,2,1:T(8,128)(2,1)}, u32[]{:S(2)}) %copy-start.1) | copy-done | bytes 1990680
  7.9 0.0 copy-start.2
  7.9 1.0 %copy-done.2 = bf16[384,384]{1,0:T(8,128)(2,1)S(1)} copy-done((bf16[384,384]{1,0:T(8,128)(2,1)S(1)}, bf16[384,384]{1,0:T(8,128)(2,1)}, u32[]{:S(2)}) %copy-start.2) | copy-done | bytes 294936
  8.8 0.0 copy-start.3
  8.8 1.0 %copy-done.3 = bf16[384,384]{1,0:T(8,128)(2,1)S(1)} copy-done((bf16[384,384]{1,0:T(8,128)(2,1)S(1)}, bf16[384,384]{1,0:T(8,128)(2,1)}, u32[]{:S(2)}) %copy-start.3) | copy-done | bytes 294936
  9.8 0.0 copy-start.4
  9.8 1.0 %copy-done.4 = bf16[384,384]{1,0:T(8,128)(2,1)S(1)} copy-done((bf16[384,384]{1,0:T(8,128)(2,1)S(1)}, bf16[384,384]{1,0:T(8,128)(2,1)}, u32[]{:S(2)}) %copy-start.4) | copy-done | bytes 294936
  10.8 0.0 copy-start.5
  10.8 1.0 %copy-done.5 = bf16[384,384]{1,0:T(8,128)(2,1)S(1)} copy-done((bf16[384,384]{1,0:T(8,128)(2,1)S(1)}, bf16[384,384]{1,0:T(8,128)(2,1)}, u32[]{:S(2)}) %copy-start.5) | copy-done | bytes 294936
  11.7 0.0 copy-start.6
  11.7 0.9 %copy-done.6 = bf16[1,2,48,384]{3,2,1,0:T(8,128)(2,1)S(1)} copy-done((bf16[1,2,48,384]{3,2,1,0:T(8,128)(2,1)S(1)}, bf16[1,2,48,384]{3,2,1,0:T(8,128)(2,1)}, u32[]{:S(2)}) %copy-start.6) | copy-done | bytes 73752
  12.6 40.2 %shard_map.145 = bf16[96,384]{1,0:T(8,128)(2,1)S(1)} custom-call(bf16[96,384]{1,0:T(8,128)(2,1)S(1)} %bitcast.15, f32[1,384]{1,0:T(1,128)S(1)} %reshape.37.g1, f32[1,384]{1,0:T(1,128)S(1)} %reshape.38.s1, bf16[27,96,384]{2,1,0:T(8,128)(2,1)S(1)} %bitcast.12, f32[1,128]{1,0:T(1,128)S(1)} %get-tuple-element.6.b1, f32[1,384]{1,0:T(1,128)S(1)} %reshape.41.g2, ...), custom_call_target="tpu_custom_call" | custom-call | tf_op jit(solution)/shard_map/pallas_call | solution.py:410
  52.8 0.6 %copy.17 = bf16[1,2,48,384]{3,2,1,0:T(8,128)(2,1)} copy(bf16[1,2,48,384]{3,2,1,0:T(8,128)(2,1)S(1)} %bitcast.14) | data formatting | bytes 147456
Async XLA Ops:
  4.8 1.6 %copy-start = (bf16[96,3,3,3,384]{4,0,3,2,1:T(8,128)(2,1)S(1)}, bf16[96,3,3,3,384]{4,0,3,2,1:T(8,128)(2,1)}, u32[]{:S(2)}) copy-start(bf16[96,3,3,3,384]{4,0,3,2,1:T(8,128)(2,1)} %param.18) | copy-start | bytes 5971972
  6.3 1.6 %copy-start.1 = (bf16[96,3,3,3,384]{4,0,3,2,1:T(8,128)(2,1)S(1)}, bf16[96,3,3,3,384]{4,0,3,2,1:T(8,128)(2,1)}, u32[]{:S(2)}) copy-start(bf16[96,3,3,3,384]{4,0,3,2,1:T(8,128)(2,1)} %param.22) | copy-start | bytes 5971972
  7.9 1.0 %copy-start.2 = (bf16[384,384]{1,0:T(8,128)(2,1)S(1)}, bf16[384,384]{1,0:T(8,128)(2,1)}, u32[]{:S(2)}) copy-start(bf16[384,384]{1,0:T(8,128)(2,1)} %wqh.1) | copy-start | bytes 884740
  8.8 1.0 %copy-start.3 = (bf16[384,384]{1,0:T(8,128)(2,1)S(1)}, bf16[384,384]{1,0:T(8,128)(2,1)}, u32[]{:S(2)}) copy-start(bf16[384,384]{1,0:T(8,128)(2,1)} %wkh.1) | copy-start | bytes 884740
  9.8 1.0 %copy-start.4 = (bf16[384,384]{1,0:T(8,128)(2,1)S(1)}, bf16[384,384]{1,0:T(8,128)(2,1)}, u32[]{:S(2)}) copy-start(bf16[384,384]{1,0:T(8,128)(2,1)} %wvh.1) | copy-start | bytes 884740
  10.8 1.0 %copy-start.5 = (bf16[384,384]{1,0:T(8,128)(2,1)S(1)}, bf16[384,384]{1,0:T(8,128)(2,1)}, u32[]{:S(2)}) copy-start(bf16[384,384]{1,0:T(8,128)(2,1)} %woh.1) | copy-start | bytes 884740
  11.7 0.9 %copy-start.6 = (bf16[1,2,48,384]{3,2,1,0:T(8,128)(2,1)S(1)}, bf16[1,2,48,384]{3,2,1,0:T(8,128)(2,1)}, u32[]{:S(2)}) copy-start(bf16[1,2,48,384]{3,2,1,0:T(8,128)(2,1)} %param.15) | copy-start | bytes 221188

commit v2 on v1

--- a/solution.py
+++ b/solution.py
@@ -14,6 +14,16 @@
 F32 = jnp.float32
 BF16 = jnp.bfloat16
 NT = (((1,), (1,)), ((), ()))
+
+
+def flat(ref):
+    return ref[...].reshape(1, ref.shape[0])
+
+
+def padded(ref):
+    row = flat(ref)
+    rest = LANES - ref.shape[0]
+    return jnp.concatenate([row, jnp.zeros((1, rest), F32)], axis=1) if rest else row
 
 
 def each(count, body):
@@ -62,9 +72,9 @@
 
 
 def kernel(T, R, W, rows, C, OUT,
-           feat, g1, s1, w1h, b1, g2, s2, w2h, b2, g3, s3, wqh, wkh, wvh, woh,
+           feath, g1h, s1h, w1h, b1h, g2h, s2h, w2h, b2h, g3h, s3h, wqh, wkh, wvh, woh,
            out,
-           xin, y1, cols, w1, w2, aw, st1, st2, hs, hfull, normed,
+           feat, g1, s1, g2, s2, g3, s3, b1, b2, xin, y1, cols, w1, w2, aw, st1, st2, hs, hfull, normed,
            lsem, blk_s, blk_r, top_s, top_r, bot_s, bot_r, st_s, st_r, hid_s, hid_r):
     t = lax.axis_index("tm")
     z = lax.axis_index("rows")
@@ -82,7 +92,13 @@
         pltpu.make_async_copy(src, aw.at[n], lsem.at[2 + n])
         for n, src in enumerate((wqh, wkh, wvh, woh))
     ]
-    for load in loads:
+    small = [
+        pltpu.make_async_copy(src, dst, lsem.at[6 + n])
+        for n, (src, dst) in enumerate((
+            (feath, feat), (g1h, g1), (s1h, s1), (g2h, g2), (s2h, s2), (g3h, g3), (s3h, s3),
+            (b1h, b1), (b2h, b2)))
+    ]
+    for load in small + loads:
         load.start()
 
     def peer(p):
@@ -102,6 +118,8 @@
             src_ref=src, dst_ref=dst, send_sem=ssem, recv_sem=rsem,
             device_id={"tm": pt, "rows": pz}, device_id_type=MESH)
 
+    for load in small:
+        load.wait()
     x = feat[...].astype(F32)
     member = membership(C, per)
     mean, square = block_stats([x], member, entries)
@@ -121,57 +139,83 @@
         src = pt * R + pz
         return remote(ref.at[src], ref.at[src], st_s.at[phase, n], st_r.at[phase, src], pt, pz)
 
-    def gather_start(phase, body, first, last, at):
-        def send_block(n):
-            pt = lax.rem(t + n + 1, T)
-            remote(body, at(t, W, RP), blk_s.at[phase, n], blk_r.at[phase, t], pt, z).start()
-
-        def send_down(n):
-            pt = lax.rem(t + n, T)
-            remote(last, at(t, 0, W), top_s.at[phase, n], top_r.at[phase, t], pt, z + 1).start()
-
-        def send_up(n):
-            pt = lax.rem(t + n, T)
-            remote(first, at(t, W + RP, W), bot_s.at[phase, n], bot_r.at[phase, t], pt, z - 1).start()
-
-        each(T - 1, send_block)
+    core = lax.rem(t, 2)
+    sib = t + 1 - 2 * core
+    X = T // 2
+    chip = t // 2
+
+    def same(n):
+        return 2 * lax.rem(chip + n, X) + core
+
+    def other(n):
+        return 2 * lax.rem(chip + n, X) + 1 - core
+
+    def pieces(phase, body, first, last, at):
+        blocks = [remote(body, at(t, W, RP), blk_s.at[phase, n], blk_r.at[phase, t], same(n), z)
+                  for n in range(1, X)]
+        blocks.append(remote(body, at(t, W, RP), blk_s.at[phase, 0], blk_r.at[phase, t], sib, z))
+        down = [remote(last, at(t, 0, W), top_s.at[phase, n], top_r.at[phase, t], same(n), z + 1)
+                for n in range(X)]
+        up = [remote(first, at(t, W + RP, W), bot_s.at[phase, n], bot_r.at[phase, t], same(n), z - 1)
+              for n in range(X)]
+        return blocks, down, up
+
+    def gather_start(*args):
+        blocks, down, up = pieces(*args)
+        for c in blocks:
+            c.start()
 
         @pl.when(z + 1 < R)
         def _():
-            each(T, send_down)
+            for c in down[1:] + down[:1]:
+                c.start()
 
         @pl.when(z > 0)
         def _():
-            each(T, send_up)
-
-    def gather_sent(phase, body, first, last, at):
-        each(T - 1, lambda n: remote(
-            body, at(t, W, RP), blk_s.at[phase, n], blk_r.at[phase, t],
-            lax.rem(t + n + 1, T), z).wait_send())
+            for c in up[1:] + up[:1]:
+                c.start()
+
+    def forward(phase, at, sems, offset, count, src, n):
+        ssem, rsem = sems
+        return remote(at(src, offset, count), at(src, offset, count),
+                      ssem.at[phase, X + n], rsem.at[phase, src], sib, z)
+
+    blk, top, bot = (blk_s, blk_r), (top_s, top_r), (bot_s, bot_r)
+    forwards = ((blk, W, RP, 1), (top, 0, W, 0), (bot, W + RP, W, 0))
+
+    def relay(phase, at, which):
+        sems, offset, count, start = forwards[which]
+        for n in range(start, X):
+            c = forward(phase, at, sems, offset, count, same(n), n)
+            c.wait_recv()
+            c.start()
+
+    def sibling_wait(phase, at, which):
+        sems, offset, count, _ = forwards[which]
+        for n in range(X):
+            forward(phase, at, sems, offset, count, other(n), n).wait_recv()
+
+    def gather_sent(*args):
+        phase, at = args[0], args[4]
+        blocks, down, up = pieces(*args)
+        for c in blocks:
+            c.wait_send()
+        for n in range(1, X):
+            forward(phase, at, blk, W, RP, same(n), n).wait_send()
 
         @pl.when(z + 1 < R)
         def _():
-            each(T, lambda n: remote(
-                last, at(t, 0, W), top_s.at[phase, n], top_r.at[phase, t],
-                lax.rem(t + n, T), z + 1).wait_send())
+            for c in down:
+                c.wait_send()
+            for n in range(X):
+                forward(phase, at, bot, W + RP, W, same(n), n).wait_send()
 
         @pl.when(z > 0)
         def _():
-            each(T, lambda n: remote(
-                first, at(t, W + RP, W), bot_s.at[phase, n], bot_r.at[phase, t],
-                lax.rem(t + n, T), z - 1).wait_send())
-
-    def block_wait(phase, at, n):
-        src = lax.rem(t + n, T)
-        remote(at(src, W, RP), at(src, W, RP), blk_s.at[phase, 0], blk_r.at[phase, src], src, z).wait_recv()
-
-    def top_wait(phase, at, n):
-        src = lax.rem(t + n, T)
-        remote(at(src, 0, W), at(src, 0, W), top_s.at[phase, 0], top_r.at[phase, src], src, z - 1).wait_recv()
-
-    def bot_wait(phase, at, n):
-        src = lax.rem(t + n, T)
-        remote(at(src, W + RP, W), at(src, W + RP, W), bot_s.at[phase, 0], bot_r.at[phase, src], src, z + 1).wait_recv()
+            for c in up:
+                c.wait_send()
+            for n in range(X):
+                forward(phase, at, top, 0, W, same(n), n).wait_send()
 
     def put_columns(f, offset, value):
         count = value.shape[0]
@@ -217,7 +261,7 @@
     xin[t, W : W + RP, :] = feat[...]
     each(N - 1, lambda n: stat_arrival(0, st1, n).wait_recv())
 
-    gain1, shift1 = g1[...], s1[...]
+    gain1, shift1 = flat(g1), flat(s1)
 
     def norm1(f):
         means = [st1[f * R + r, 0:1, :] for r in range(R)]
@@ -230,19 +274,28 @@
         value = (xin[f, pl.ds(offset, count), :].astype(F32) - mean) * scale + shift1
         put_columns(f, offset, value)
 
-    def body1(n):
-        if n > 0:
-            block_wait(0, at1, n)
-        fill1(lax.rem(t + n, T), W, RP)
-
-    for n in range(T):
-        body1(n)
+    fill1(t, W, RP)
+    relay(0, at1, 0)
 
     @pl.when(z > 0)
     def _():
-        for n in range(T):
-            top_wait(0, at1, n)
-            fill1(lax.rem(t + n, T), 0, W)
+        relay(0, at1, 1)
+
+    @pl.when(z + 1 < R)
+    def _():
+        relay(0, at1, 2)
+
+    for n in range(1, X):
+        fill1(same(n), W, RP)
+    sibling_wait(0, at1, 0)
+    for n in range(X):
+        fill1(other(n), W, RP)
+
+    @pl.when(z > 0)
+    def _():
+        sibling_wait(0, at1, 1)
+        for f in range(T):
+            fill1(f, 0, W)
 
     @pl.when(z == 0)
     def _():
@@ -251,9 +304,9 @@
 
     @pl.when(z + 1 < R)
     def _():
-        for n in range(T):
-            bot_wait(0, at1, n)
-            fill1(lax.rem(t + n, T), W + RP, W)
+        sibling_wait(0, at1, 2)
+        for f in range(T):
+            fill1(f, W + RP, W)
 
     @pl.when(z + 1 == R)
     def _():
@@ -261,7 +314,7 @@
             cols[f, W + RP : EXT, :] = zero_row
 
     loads[0].wait()
-    bias1 = b1[...]
+    bias1 = padded(b1)
     outs = [(v + bias1).astype(BF16) for v in conv(w1)]
     member_out = membership(LANES, per)
     for f in range(T):
@@ -282,7 +335,7 @@
     own = jnp.dot(xin[:, W : W + RP, :].reshape(T * RP, C), pick, preferred_element_type=F32)
 
     each(N - 1, lambda n: stat_arrival(1, st2, n).wait_recv())
-    gain2, shift2 = g2[...], s2[...]
+    gain2, shift2 = flat(g2), flat(s2)
     mean_cols, inv_cols = [], []
     for s in range(T):
         mean, inv = merge_stats(
@@ -300,42 +353,85 @@
         value = (raw - mean2[f : f + 1]) * scale2[f : f + 1] + shift2
         put_columns(f, offset, value)
 
-    for n in range(1, T):
-        block_wait(1, at2, n)
+    relay(1, at2, 0)
+
+    @pl.when(z > 0)
+    def _():
+        relay(1, at2, 1)
+
+    @pl.when(z + 1 < R)
+    def _():
+        relay(1, at2, 2)
+
+    sibling_wait(1, at2, 0)
     for f in range(T):
         fill2(f, W, RP)
 
     @pl.when(z > 0)
     def _():
-        for n in range(T):
-            top_wait(1, at2, n)
+        sibling_wait(1, at2, 1)
         for f in range(T):
             fill2(f, 0, W)
 
     @pl.when(z + 1 < R)
     def _():
-        for n in range(T):
-            bot_wait(1, at2, n)
+        sibling_wait(1, at2, 2)
         for f in range(T):
             fill2(f, W + RP, W)
 
     loads[1].wait()
-    bias2 = b2[...]
+    bias2 = padded(b2)
     for f, v in enumerate(conv(w2)):
         rounded = (v + bias2).astype(BF16).astype(F32)
         hs[f] = (own[f * RP : (f + 1) * RP] + rounded).astype(BF16)
 
+    def place(src, zz):
+        return hfull.at[src, pl.ds(pl.multiple_of(zz * RP, 16), RP), :]
+
     def hidden_copy(n):
-        pt, pz = peer(n + 1)
-        return remote(hs.at[pt], hfull.at[t, pl.ds(z * RP, RP), :], hid_s.at[n], hid_r.at[me], pt, pz)
-
-    def hidden_arrival(n):
-        pt, pz = peer(n + 1)
-        dst = hfull.at[pt, pl.ds(pz * RP, RP), :]
-        return remote(dst, dst, hid_s.at[n], hid_r.at[pt * R + pz], pt, pz)
-
-    each(N - 1, lambda n: hidden_copy(n).start())
-    hfull[t, pl.ds(z * RP, RP), :] = hs[t]
+        pt = lax.rem(t + n + 1, T)
+        return remote(hs.at[pt], place(t, z), hid_s.at[2, n], hid_r.at[me], pt, z)
+
+    def passed(way, src, zz):
+        return remote(place(src, zz), place(src, zz), hid_s.at[way, src * R + zz],
+                      hid_r.at[src * R + zz], t, z + 1 if way == 0 else z - 1)
+
+    def along(act, begin):
+        def step(m):
+            d = m + begin
+
+            @pl.when(z - d >= 0)
+            def _():
+                for n in range(T):
+                    act(lax.rem(t + n, T), z - d, 0)
+
+            @pl.when(z + d < R)
+            def _():
+                for n in range(T):
+                    act(lax.rem(t + n, T), z + d, 1)
+
+        each(R - begin, step)
+
+    each(T - 1, lambda n: hidden_copy(n).start())
+    hfull[t, pl.ds(pl.multiple_of(z * RP, 16), RP), :] = hs[t]
+
+    def onward(src, zz, way):
+        @pl.when(z + 1 < R if way == 0 else z > 0)
+        def _():
+            passed(way, src, zz).start()
+
+    for n in range(T):
+        src = lax.rem(t + n, T)
+        if n > 0:
+            passed(0, src, z).wait_recv()
+        onward(src, z, 0)
+        onward(src, z, 1)
+
+    def arrive(src, zz, way):
+        passed(way, src, zz).wait_recv()
+        onward(src, zz, way)
+
+    along(arrive, 1)
 
     each(N - 1, lambda n: stat_copy(0, st1, n).wait_send())
     gather_sent(*phase1)
@@ -344,8 +440,6 @@
     for n in range(2, 6):
         loads[n].wait()
 
-    each(N - 1, lambda n: hidden_arrival(n).wait_recv())
-
     total_rows = R * RP
     chunk = min(total_rows, 4 * RP)
     parts = total_rows // chunk
@@ -368,8 +462,8 @@
         return a + jnp.sum(d * d, axis=0, keepdims=True)
 
     var = group_sum(fold(deviation, zero), member) / (entries * R)
-    scale3 = lax.rsqrt(var + EPS) * g3[...]
-    shift3 = s3[...]
+    scale3 = lax.rsqrt(var + EPS) * flat(g3)
+    shift3 = flat(s3)
 
     def normalise(n, c):
         start = pl.multiple_of(n * chunk, 16)
@@ -391,7 +485,17 @@
     hidden = joined([hfull[s, mine, :] for s in range(T)])
     out[...] = (hidden + jnp.dot(attended, aw[3], preferred_element_type=F32)).astype(BF16)
 
-    each(N - 1, lambda n: hidden_copy(n).wait_send())
+    each(T - 1, lambda n: hidden_copy(n).wait_send())
+
+    def left(src, zz, way):
+        @pl.when(z + 1 < R if way == 0 else z > 0)
+        def _():
+            passed(way, src, zz).wait_send()
+
+    for n in range(T):
+        left(lax.rem(t + n, T), z, 0)
+        left(lax.rem(t + n, T), z, 1)
+    along(left, 1)
 
 
 def solution(mesh):
@@ -401,18 +505,17 @@
         _, rows, W, C = features.shape
         OUT = k1.shape[0]
         RP, EXT, N = rows * W, (rows + 2) * W, T * R
-        vec = lambda a: a.reshape(1, -1)
-        pad = lambda a: jnp.pad(a, (0, LANES - OUT)).reshape(1, LANES)
         taps = lambda k: jnp.transpose(k, (1, 2, 3, 0, 4)).reshape(27, OUT, C)
         vmem = pl.BlockSpec(memory_space=pltpu.VMEM)
-        hbm = pl.BlockSpec(memory_space=pl.ANY)
+        hbm = pl.BlockSpec(memory_space=pltpu.HBM)
         dma = pltpu.SemaphoreType.DMA
         result = pl.pallas_call(
             functools.partial(kernel, T, R, W, rows, C, OUT),
             out_shape=jax.ShapeDtypeStruct((RP, C), BF16),
-            in_specs=[vmem, vmem, vmem, hbm, vmem, vmem, vmem, hbm, vmem, vmem, vmem, hbm, hbm, hbm, hbm],
+            in_specs=[hbm] * 15,
             out_specs=vmem,
-            scratch_shapes=[
+            scratch_shapes=[pltpu.VMEM((RP, C), BF16)] + [pltpu.VMEM((C,), F32)] * 6
+            + [pltpu.VMEM((OUT,), F32)] * 2 + [
                 pltpu.VMEM((T, EXT, C), BF16),
                 pltpu.VMEM((T, T, EXT, LANES), BF16),
                 pltpu.VMEM((T, EXT, 3 * C), BF16),
@@ -424,17 +527,17 @@
                 pltpu.VMEM((T, RP, LANES), BF16),
                 pltpu.VMEM((T, R * RP, LANES), BF16),
                 pltpu.VMEM((3, R * RP, C), BF16),
-                dma((6,)),
+                dma((15,)),
                 dma((2, T)), dma((2, T)),
                 dma((2, T)), dma((2, T)),
                 dma((2, T)), dma((2, T)),
                 dma((2, N)), dma((2, N)),
-                dma((N,)), dma((N,)),
+                dma((3, N)), dma((N,)),
             ],
             compiler_params=pltpu.CompilerParams(
-                collective_id=0, has_side_effects=True, vmem_limit_bytes=48 * 1024 * 1024),
-        )(features.reshape(RP, C), vec(g1), vec(s1), taps(k1), pad(b1), vec(g2), vec(s2),
-          taps(k2), pad(b2), vec(g3), vec(s3), wq, wk, wv, wo)
+                collective_id=0, has_side_effects=True, vmem_limit_bytes=62 * 1024 * 1024),
+        )(features.reshape(RP, C), g1, s1, taps(k1), b1, g2, s2,
+          taps(k2), b2, g3, s3, wq, wk, wv, wo)
         return result.reshape(features.shape)
 
     in_specs = (

time: 54 us -> 44.1 us (0.82)
  local copies, waits for them, and re-layouts: 13.2 us -> 1.52 us
  Pallas kernels: 40.2 us -> 42.4 us
    unnamed x15 -> x1, local copies, waits for them, and re-layouts: 8.47 us -> 1.52 us
    reshape x7 -> x0, local copies, waits for them, and re-layouts: 4.77 us -> none  [the longest x6 4.1 us: per_device(): vec = lambda a: a.reshape(1, -1)]
    pallas_call x1, Pallas kernels: 40.2 us -> 42.4 us  [per_device(): pl.pallas_call(functools.partial(kernel, T, R, W, rows, C, OUT), out_shap...]
where the time goes in v2:
time: 44.1 us; the launch traced here: 44 us
  Pallas kernels  42.4 us (96%)
  local copies, waits for them, and re-layouts  1.52 us (3%)
    pallas_call x1, Pallas kernels, per_device(): pl.pallas_call(functools.partial(kernel, T, R, W, rows, C, OUT), out_shap...  42.4 us
    unnamed x1, local copies, waits for them, and re-layouts  1.52 us

profile of v2, /device:TPU:0, one launch (start us, length us, event | category | flops | bytes accessed | tf_op | source)
XLA Modules:
  0.0 44.0 jit_solution(15897059865375338697)
XLA Ops:
  0.0 42.4 %shard_map.145 = bf16[96,384]{1,0:T(8,128)(2,1)} custom-call(bf16[96,384]{1,0:T(8,128)(2,1)} %bitcast.11, f32[384]{0:T(512)} %g1h.1, f32[384]{0:T(512)} %s1h.1, bf16[27,96,384]{2,1,0:T(8,128)(2,1)} %bitcast.8, f32[96]{0:T(128)} %b1h.1, f32[384]{0:T(512)} %g2h.1, f32[384]{0:T(512)} %s2h.1, bf16[27,96,384]{2,1,0:T(8,128)(2,1)} %bitcast.9, f32[96]{0:T(128)} %b2h.1, ...), custom_call_target="tpu_custom_call" | custom-call | tf_op jit(solution)/shard_map/pallas_call | solution.py:512
  42.4 1.5 %copy.17 = bf16[1,2,48,384]{3,2,1,0:T(8,128)(2,1)} copy(bf16[1,2,48,384]{3,2,1,0:T(8,128)(2,1)} %bitcast.10) | data formatting | bytes 147456

commit v3 on v2

--- a/solution.py
+++ b/solution.py
@@ -389,49 +389,15 @@
         return hfull.at[src, pl.ds(pl.multiple_of(zz * RP, 16), RP), :]
 
     def hidden_copy(n):
-        pt = lax.rem(t + n + 1, T)
-        return remote(hs.at[pt], place(t, z), hid_s.at[2, n], hid_r.at[me], pt, z)
-
-    def passed(way, src, zz):
-        return remote(place(src, zz), place(src, zz), hid_s.at[way, src * R + zz],
-                      hid_r.at[src * R + zz], t, z + 1 if way == 0 else z - 1)
-
-    def along(act, begin):
-        def step(m):
-            d = m + begin
-
-            @pl.when(z - d >= 0)
-            def _():
-                for n in range(T):
-                    act(lax.rem(t + n, T), z - d, 0)
-
-            @pl.when(z + d < R)
-            def _():
-                for n in range(T):
-                    act(lax.rem(t + n, T), z + d, 1)
-
-        each(R - begin, step)
-
-    each(T - 1, lambda n: hidden_copy(n).start())
+        pt, pz = peer(n + 1)
+        return remote(hs.at[pt], place(t, z), hid_s.at[n], hid_r.at[me], pt, pz)
+
+    def hidden_arrival(n):
+        pt, pz = peer(n + 1)
+        return remote(place(pt, pz), place(pt, pz), hid_s.at[n], hid_r.at[pt * R + pz], pt, pz)
+
+    each(N - 1, lambda n: hidden_copy(n).start())
     hfull[t, pl.ds(pl.multiple_of(z * RP, 16), RP), :] = hs[t]
-
-    def onward(src, zz, way):
-        @pl.when(z + 1 < R if way == 0 else z > 0)
-        def _():
-            passed(way, src, zz).start()
-
-    for n in range(T):
-        src = lax.rem(t + n, T)
-        if n > 0:
-            passed(0, src, z).wait_recv()
-        onward(src, z, 0)
-        onward(src, z, 1)
-
-    def arrive(src, zz, way):
-        passed(way, src, zz).wait_recv()
-        onward(src, zz, way)
-
-    along(arrive, 1)
 
     each(N - 1, lambda n: stat_copy(0, st1, n).wait_send())
     gather_sent(*phase1)
@@ -439,6 +405,8 @@
     gather_sent(*phase2)
     for n in range(2, 6):
         loads[n].wait()
+
+    each(N - 1, lambda n: hidden_arrival(n).wait_recv())
 
     total_rows = R * RP
     chunk = min(total_rows, 4 * RP)
@@ -485,17 +453,7 @@
     hidden = joined([hfull[s, mine, :] for s in range(T)])
     out[...] = (hidden + jnp.dot(attended, aw[3], preferred_element_type=F32)).astype(BF16)
 
-    each(T - 1, lambda n: hidden_copy(n).wait_send())
-
-    def left(src, zz, way):
-        @pl.when(z + 1 < R if way == 0 else z > 0)
-        def _():
-            passed(way, src, zz).wait_send()
-
-    for n in range(T):
-        left(lax.rem(t + n, T), z, 0)
-        left(lax.rem(t + n, T), z, 1)
-    along(left, 1)
+    each(N - 1, lambda n: hidden_copy(n).wait_send())
 
 
 def solution(mesh):
@@ -532,7 +490,7 @@
                 dma((2, T)), dma((2, T)),
                 dma((2, T)), dma((2, T)),
                 dma((2, N)), dma((2, N)),
-                dma((3, N)), dma((N,)),
+                dma((N,)), dma((N,)),
             ],
             compiler_params=pltpu.CompilerParams(
                 collective_id=0, has_side_effects=True, vmem_limit_bytes=62 * 1024 * 1024),

time: 44.1 us -> 40.7 us (0.923)
  Pallas kernels: 42.4 us -> 39 us
    pallas_call x1, Pallas kernels: 42.4 us -> 39 us  [per_device(): pl.pallas_call(functools.partial(kernel, T, R, W, rows, C, OUT), out_shap...]
where the time goes in v3:
time: 40.7 us; the launch traced here: 40.5 us
  Pallas kernels  39 us (96%)
  local copies, waits for them, and re-layouts  1.52 us (4%)
    pallas_call x1, Pallas kernels, per_device(): pl.pallas_call(functools.partial(kernel, T, R, W, rows, C, OUT), out_shap...  39 us
    unnamed x1, local copies, waits for them, and re-layouts  1.52 us

profile of v3, /device:TPU:0, one launch (start us, length us, event | category | flops | bytes accessed | tf_op | source)
XLA Modules:
  0.0 40.5 jit_solution(6317948326270687304)
XLA Ops:
  0.0 39.0 %shard_map.145 = bf16[96,384]{1,0:T(8,128)(2,1)} custom-call(bf16[96,384]{1,0:T(8,128)(2,1)} %bitcast.11, f32[384]{0:T(512)} %g1h.1, f32[384]{0:T(512)} %s1h.1, bf16[27,96,384]{2,1,0:T(8,128)(2,1)} %bitcast.8, f32[96]{0:T(128)} %b1h.1, f32[384]{0:T(512)} %g2h.1, f32[384]{0:T(512)} %s2h.1, bf16[27,96,384]{2,1,0:T(8,128)(2,1)} %bitcast.9, f32[96]{0:T(128)} %b2h.1, ...), custom_call_target="tpu_custom_call" | custom-call | tf_op jit(solution)/shard_map/pallas_call | solution.py:470
  39.0 1.5 %copy.17 = bf16[1,2,48,384]{3,2,1,0:T(8,128)(2,1)} copy(bf16[1,2,48,384]{3,2,1,0:T(8,128)(2,1)} %bitcast.10) | data formatting | bytes 147456
